TPU v7x, 256 devices: a whole 4x4x8 slice. The times are simulated.
256 devices in a mesh: dp: 8 (over x, y_lo), seq: 32 (over z, y_hi, core).
Axes of the slice: x: 4, y: 4 (y_hi: 2, y_lo: 2; y = y_hi * 2 + y_lo), z: 8, core: 2. Of those that a mesh axis runs over, the one named last changes fastest.
Arguments:
- tokens: float32 [8, 16384, 512], P('dp', 'seq'), may hold values from -6 to 6
- in_weight: float32 [512, 1024], P('dp'), may hold values from -0.25 to 0.25
- filters: float32 [16384, 512], P('seq'), may hold values from -1.5 to 1.5
- cotangent: float32 [8, 16384, 512], P('dp', 'seq'), may hold values from -6 to 6
Outputs:
- mixed: float32 [8, 16384, 512], P('dp', 'seq')
- token_grad: float32 [8, 16384, 512], P('dp', 'seq')
- weight_grad: float32 [512, 1024], P('dp')
All inputs are finite; a program needn't handle non-finite values.
Results may differ from a plain program's by a relative error of at most 0.00011.
Values sent between devices are 32-bit elements; how exact they have to be, the bound alone decides.
A program may use at most 128 MiB of HBM per device.

v0:
```python
import math

import jax
import jax.numpy as jnp
from jax import lax
from jax.sharding import PartitionSpec as P

precise = lax.Precision.HIGHEST


def complex_mul(signal, real_part, imag_part):
    first = signal[0]
    second = signal[1]
    return jnp.stack(
        [first * real_part - second * imag_part, first * imag_part + second * real_part]
    )


def phase_pair(numer, denom, sign):
    angle_vals = sign * 2.0 * math.pi / denom * numer.astype(jnp.float32)
    return (jnp.cos(angle_vals), jnp.sin(angle_vals))


def dft_matrix(length, sign):
    index_vals = jnp.arange(length, dtype=jnp.int32)
    cosine, sine = phase_pair(index_vals[:, None] * index_vals[None, :] % length, length, sign)
    top_rows = jnp.stack([cosine, -sine], axis=1)
    bottom_rows = jnp.stack([sine, cosine], axis=1)
    return jnp.stack([top_rows, bottom_rows], axis=0)


def local_transform(signal, sign):
    matrix = dft_matrix(signal.shape[2], sign)
    return jnp.einsum("akbm,bjmc->ajkc", matrix, signal, precision=precise)


def row_twiddle(signal, freq_block, sign):
    row_count = signal.shape[2]
    total = row_count * lax.axis_size("seq")
    row_index = jnp.arange(row_count, dtype=jnp.int32)
    cosine, sine = phase_pair(row_index * freq_block % total, total, sign)
    return complex_mul(signal, cosine[None, :, None], sine[None, :, None])


def block_twiddle(moved, row_count, sign):
    count = lax.axis_size("seq")
    piece = row_count // count
    device_pos = lax.axis_index("seq")
    freq_index = jnp.arange(count, dtype=jnp.int32)[:, None]
    row_index = device_pos * piece + jnp.arange(piece, dtype=jnp.int32)[None, :]
    total = row_count * count
    cosine, sine = phase_pair(freq_index * row_index % total, total, sign)
    return complex_mul(moved, cosine[None, :, :, None], sine[None, :, :, None])


def spectral_mix(spectra, seq_count):
    value_spec = spectra[:, :seq_count]
    conv_spec = spectra[:, seq_count : 2 * seq_count]
    filter_real = spectra[0, 2 * seq_count][None]
    filter_imag = spectra[1, 2 * seq_count][None]
    real_out = (
        value_spec[0] * filter_real
        - value_spec[1] * filter_imag
        - conv_spec[1] * filter_real
        + conv_spec[0] * filter_imag
    )
    imag_out = (
        value_spec[0] * filter_imag
        + value_spec[1] * filter_real
        + conv_spec[0] * filter_real
        + conv_spec[1] * filter_imag
    )
    return jnp.stack([real_out, imag_out])


def forward_spread(signal):
    count = lax.axis_size("seq")
    row_count = signal.shape[1]
    moved = lax.all_to_all(signal[:, None], "seq", split_axis=2, concat_axis=1, tiled=True)
    matrix = dft_matrix(count, -1.0)[:, :, 0]
    moved = jnp.einsum("akp,jpmc->ajkmc", matrix, moved, precision=precise)
    moved = block_twiddle(moved, row_count, -1.0)
    returned = lax.all_to_all(moved, "seq", split_axis=2, concat_axis=3, tiled=True)
    return local_transform(returned[:, :, 0], -1.0)


def inverse_spread(signal):
    count = lax.axis_size("seq")
    row_count = signal.shape[2]
    signal = local_transform(signal, 1.0)
    signal = row_twiddle(signal, lax.axis_index("seq"), 1.0)
    moved = lax.all_to_all(signal[:, :, None], "seq", split_axis=3, concat_axis=2, tiled=True)
    moved = jnp.einsum("akbp,bjpmc->ajkmc", dft_matrix(count, 1.0), moved, precision=precise)
    returned = lax.all_to_all(moved, "seq", split_axis=2, concat_axis=3, tiled=True)
    return returned[:, :, 0] / (row_count * count)


def spread_convolve(real_rows, seq_count):
    spectra = forward_spread(real_rows)
    results = inverse_spread(spectral_mix(spectra, seq_count))
    return (results[0], results[1])


def shards(tokens, in_weight, filters, cotangent):
    seq_count, row_count, channels = tokens.shape
    weights = lax.all_gather(in_weight, "dp", axis=0, tiled=True)
    flat_tokens = tokens.reshape(seq_count * row_count, channels)
    projected = jnp.dot(flat_tokens, weights, precision=precise, preferred_element_type=jnp.float32)
    projected = projected.reshape(seq_count, row_count, 2 * channels)
    value_part = projected[..., :channels]
    gate_part = projected[..., channels:]
    d_conv = cotangent * gate_part
    real_rows = jnp.concatenate([value_part, d_conv, filters[None]], axis=0)
    convolved, d_value = spread_convolve(real_rows, seq_count)
    mixed = gate_part * convolved
    d_gate = cotangent * convolved
    d_pre = jnp.concatenate([d_value, d_gate], axis=2).reshape(seq_count * row_count, 2 * channels)
    token_grad = lax.dot_general(
        d_pre,
        weights,
        (((1,), (1,)), ((), ())),
        precision=precise,
        preferred_element_type=jnp.float32,
    )
    local_grad = lax.dot_general(
        flat_tokens,
        d_pre,
        (((0,), (0,)), ((), ())),
        precision=precise,
        preferred_element_type=jnp.float32,
    )
    grad_shard = lax.psum_scatter(local_grad, "dp", scatter_dimension=0, tiled=True)
    grad_total = lax.psum(grad_shard, "seq")
    token_total = seq_count * lax.axis_size("dp") * row_count * lax.axis_size("seq")
    weight_grad = grad_total * (1.0 / math.sqrt(token_total))
    return (mixed, token_grad.reshape(seq_count, row_count, channels), weight_grad)


def solution(mesh):
    placed = (P("dp", "seq", None), P("dp", None), P("seq", None), P("dp", "seq", None))
    return jax.shard_map(
        shards,
        mesh=mesh,
        in_specs=placed,
        out_specs=(P("dp", "seq", None), P("dp", "seq", None), P("dp", None)),
        check_vma=False,
    )
```

profile of v0, /device:TPU:1, one launch (start us, length us, event | category | flops | bytes accessed | tf_op | source)
XLA Modules:
  0.0 859.4 jit_solution(12314258488869934465)
XLA Ops:
  7.9 58.7 %all-gather.2.cloned.1.call-done = f32[512,1024]{1,0:T(8,128)} async-done(((f32[64,1024]{1,0:T(8,128)}), f32[512,1024]{1,0:T(8,128)}) %all-gather.2.cloned.1.call-update) | async-done | bytes 2097168 | tf_op jit(solution)/shard_map/all_gather | solution.py:106
  66.6 5.2 convolution_bitcast_fusion
  73.4 4.9 copy.44
  78.3 10.9 %all-to-all-start = ((f32[3,1,512,512]{3,1,0,2:T(1,128)}), f32[3,1,512,512]{3,1,0,2:T(1,128)}, u32[]{:S(2)}, u32[]{:S(2)}) async-start(f32[3,1,512,512]{3,1,0,2:T(1,128)} %copy.44), calls=%async_computation | async-start | bytes 6291456 | tf_op jit(solution)/shard_map/all_to_all | solution.py:79
  89.5 73.6 %all-to-all-done = f32[3,1,512,512]{3,1,0,2:T(1,128)} async-done(((f32[3,1,512,512]{3,1,0,2:T(1,128)}), f32[3,1,512,512]{3,1,0,2:T(1,128)}, u32[]{:S(2)}, u32[]{:S(2)}) %all-to-all-start) | async-done | bytes 3145760 | tf_op jit(solution)/shard_map/all_to_all | solution.py:79
  165.4 8.0 fusion.10
  178.4 10.5 %copy.48 = f32[2,3,32,16,512]{4,0,3,1,2:T(2,128)} copy(f32[2,3,32,16,512]{4,2,0,3,1:T(8,128)} %pad_maximum_fusion) | data formatting | bytes 12582912 | tf_op jit(solution)/shard_map/stack | solution.py:14
  188.9 5.0 all-to-all-start.1
  197.8 3.9 fusion.35
  201.6 4.6 multiply_sine_fusion.1
  206.2 4.1 multiply_sine_fusion
  215.5 120.1 %all-to-all-done.1 = f32[2,3,32,16,512]{4,0,3,1,2:T(2,128)} async-done(((f32[2,3,32,16,512]{4,0,3,1,2:T(2,128)}), f32[2,3,32,16,512]{4,0,3,1,2:T(2,128)}, u32[]{:S(2)}, u32[]{:S(2)}) %all-to-all-start.1) | async-done | bytes 6291488 | tf_op jit(solution)/shard_map/all_to_all | solution.py:83
  335.6 4.1 copy.73
  339.7 40.7 %fusion.9 = f32[2,3,512,512]{2,3,0,1:T(8,128)S(1)} fusion(f32[2,3,512,512,1]{3,2,0,4,1:T(8,128)S(1)} %bitcast.101, f32[1,512,2,512]{3,1,2,0:T(8,128)S(1)} %copy-done.8, f32[1,512,2,512]{3,1,2,0:T(8,128)S(1)} %copy-done.7), kind=kOutput, calls=%fused_computation.14 | convolution fusion | flops 19328401408 | bytes 16777216 | tf_op jit(solution)/shard_map/akbm,bjmc->ajkc/dot_general | solution.py:34
  382.7 6.9 fusion.23
  391.4 4.1 copy.51
  395.5 5.0 all-to-all-start.2
  400.7 49.9 %all-to-all-done.2 = f32[2,1,1,512,512]{4,0,2,1,3:T(2,128)} async-done(((f32[2,1,1,512,512]{4,0,2,1,3:T(2,128)}), f32[2,1,1,512,512]{4,0,2,1,3:T(2,128)}, u32[]{:S(2)}, u32[]{:S(2)}) %all-to-all-start.2) | async-done | bytes 2097184 | tf_op jit(solution)/shard_map/all_to_all | solution.py:92
  450.6 4.9 fusion.20
  457.1 56.9 %all_to_all.19 = f32[2,1,32,16,512]{4,0,3,1,2:T(2,128)S(1)} all-to-all(f32[2,1,32,16,512]{4,0,3,1,2:T(2,128)S(1)} %copy.54), channel_id=1, replica_groups=mesh['dp'=8,'seq'=32] {'seq'}, dimensions={2} | all-to-all | bytes 4194304 | tf_op jit(solution)/shard_map/all_to_all | solution.py:94
  521.0 4.8 fusion.19
  528.7 49.1 %reduce-scatter.4.cloned.1.call-done = f32[64,1024]{1,0:T(8,128)} async-done(((f32[512,1024]{1,0:T(8,128)}), f32[64,1024]{1,0:T(8,128)}) %reduce-scatter.4.cloned.1.call-update) | async-done | bytes 262160
  579.8 6.1 fusion.26
  585.9 264.8 %all-reduce.2.cloned.1.call-done = f32[64,1024]{0,1:T(8,128)} async-done(((f32[64,1024]{0,1:T(8,128)}), f32[64,1024]{0,1:T(8,128)}) %all-reduce.2.cloned.1.call-update) | async-done | bytes 262160 | tf_op jit(solution)/shard_map/psum | solution.py:133
  (56 shorter events, 38.5 us)
Async XLA Ops:
  7.2 59.4 %copy-start = (f32[1,512,512]{2,1,0:T(8,128)S(1)}, f32[1,512,512]{2,1,0:T(8,128)}, u32[]{:S(2)}) copy-start(f32[1,512,512]{2,1,0:T(8,128)} %param.4) | copy-start | bytes 3145732
  7.2 59.4 %all-gather.2.cloned.1.call-start = ((), (), s32[]{:S(2)}) async-start(), calls=%async_computation.5 | async-start | bytes 2359296 | tf_op jit(solution)/shard_map/all_gather | solution.py:106
  66.6 5.2 copy-start.5
  71.8 1.2 copy-start.9
  78.3 84.8 %all-to-all-start = ((f32[3,1,512,512]{3,1,0,2:T(1,128)}), f32[3,1,512,512]{3,1,0,2:T(1,128)}, u32[]{:S(2)}, u32[]{:S(2)}) async-start(f32[3,1,512,512]{3,1,0,2:T(1,128)} %copy.44), calls=%async_computation | async-start | bytes 6291456 | tf_op jit(solution)/shard_map/all_to_all | solution.py:79
  188.9 146.7 %all-to-all-start.1 = ((f32[2,3,32,16,512]{4,0,3,1,2:T(2,128)}), f32[2,3,32,16,512]{4,0,3,1,2:T(2,128)}, u32[]{:S(2)}, u32[]{:S(2)}) async-start(f32[2,3,32,16,512]{4,0,3,1,2:T(2,128)} %copy.48), calls=%async_computation.1 | async-start | bytes 12582912 | tf_op jit(solution)/shard_map/all_to_all | solution.py:83
  335.6 4.1 copy-start.7
  335.6 4.2 copy-start.8
  380.4 1.6 copy-start.3
  380.4 2.2 copy-start.4
  395.5 55.1 %all-to-all-start.2 = ((f32[2,1,1,512,512]{4,0,2,1,3:T(2,128)}), f32[2,1,1,512,512]{4,0,2,1,3:T(2,128)}, u32[]{:S(2)}, u32[]{:S(2)}) async-start(f32[2,1,1,512,512]{4,0,2,1,3:T(2,128)} %copy.51), calls=%async_computation.2 | async-start | bytes 4194304 | tf_op jit(solution)/shard_map/all_to_all | solution.py:92
  400.5 177.3 %reduce-scatter.4.cloned.1.call-start = ((), (), s32[]{:S(2)}) async-start(), calls=%async_computation.7 | async-start | bytes 2359296
  517.4 1.2 copy-start.6
  520.0 1.0 copy-start.1
  528.7 51.1 %copy-start.2 = (f32[1,512,512]{2,1,0:T(8,128)S(1)}, f32[1,512,512]{2,1,0:T(8,128)}, u32[]{:S(2)}) copy-start(f32[1,512,512]{2,1,0:T(8,128)} %copy-done.1) | copy-start | bytes 3145732
  528.7 322.0 %all-reduce.2.cloned.1.call-start = ((), (), s32[]{:S(2)}) async-start(), calls=%async_computation.6 | async-start | bytes 1048576 | tf_op jit(solution)/shard_map/psum | solution.py:133
Sparse Core Ops, SparseCore 0:
  9.8 56.7 all-gather.1
  528.8 48.9 reduce-scatter.3
  580.4 270.1 all-reduce.1
where the time goes:
time: 866 us; the launch traced here: 859 us
  waiting for transfers between devices  617 us (71%)
  matrix products  76.7 us (9%)
  blocking collectives  56.9 us (7%)
  local copies, waits for them, and re-layouts  40.1 us (5%)
  other arithmetic  33.7 us (4%)
  starting transfers between devices  20.9 us (2%)
  between operations  14.2 us (2%)
    psum x1, waiting for transfers between devices, shards(): grad_total = lax.psum(grad_shard, 'seq')  265 us
    all_to_all x1, waiting for transfers between devices, forward_spread(): lax.all_to_all(moved, 'seq', split_axis=2, concat_axis=3, tiled=True)  120 us
    all_to_all x1, waiting for transfers between devices, forward_spread(): lax.all_to_all(signal[:, None], 'seq', split_axis=2, concat_axis=1, tiled...  73.6 us
    all_gather x1, waiting for transfers between devices, shards(): weights = lax.all_gather(in_weight, 'dp', axis=0, tiled=True)  58.7 us
    all_to_all x1, blocking collectives, inverse_spread(): lax.all_to_all(moved, 'seq', split_axis=2, concat_axis=3, tiled=True)  56.9 us
    all_to_all x1, waiting for transfers between devices, inverse_spread(): lax.all_to_all(signal[:, :, None], 'seq', split_axis=3, concat_axis=2, ti...  49.9 us
    unnamed x4, waiting for transfers between devices  49.8 us
    dot_general x2, matrix products, local_transform(): return jnp.einsum('akbm,bjmc->ajkc', matrix, signal, precision=precise)  47.6 us
  transfers between devices with their start and end apart: 6, of which 6 were waited for; matrix products, arithmetic and copies ran while one was open for 3% of the time, Pallas kernels for 0%

commit v1 on v0

v1 whole, which is shorter than its diff:
```python
import math

import jax
import jax.numpy as jnp
import numpy as np
from jax import lax
from jax.experimental import pallas as pl
from jax.experimental.pallas import tpu as pltpu
from jax.sharding import PartitionSpec as P

F32 = jnp.float32
BF16 = jnp.bfloat16
MESH = pl.DeviceIdType.MESH
CORES = 2
QUARTER = 4
CHUNK_CHANNELS = 4


def split_np(values):
    high = values.astype(np.float32).astype(jnp.bfloat16)
    low = (values - high.astype(np.float64)).astype(np.float32).astype(jnp.bfloat16)
    return high, low


def trig(rows, columns, period):
    product = np.outer(np.arange(rows), np.arange(columns)) % period
    angle = 2.0 * np.pi * product / period
    return np.cos(angle), np.sin(angle)


def tables(seq, lanes):
    n1 = QUARTER * seq
    total = n1 * lanes
    c1, s1 = trig(n1, n1, n1)
    c2, s2 = trig(lanes, lanes, lanes)
    ct, st = trig(n1, lanes, total)
    n1_of = np.arange(n1).reshape(seq, QUARTER)
    zeros = np.zeros((n1, seq, QUARTER))
    top_v = np.concatenate([c1[:, n1_of], zeros], axis=2).reshape(n1, 2 * n1)
    bot_v = np.concatenate([-s1[:, n1_of], zeros], axis=2).reshape(n1, 2 * n1)
    top_d = np.concatenate([zeros, c1[:, n1_of]], axis=2).reshape(n1, 2 * n1)
    bot_d = np.concatenate([zeros, s1[:, n1_of]], axis=2).reshape(n1, 2 * n1)
    forward1 = np.concatenate([top_v, bot_v, top_d, bot_d], axis=0)
    forward_re = np.concatenate([c2, s2], axis=0)
    forward_im = np.concatenate([c2, -s2], axis=0)
    filter2 = np.block([[c2, -s2], [s2, c2]])
    inverse2 = np.block([[c2, s2, c2, -s2], [-s2, c2, s2, c2]])
    zero = np.zeros((n1, n1))
    conv_rows = np.concatenate([c1, -s1, zero, zero], axis=1) / total
    value_rows = np.concatenate([zero, zero, -s1, c1], axis=1) / total
    inverse1 = np.stack(
        [conv_rows.reshape(seq, QUARTER, 4 * n1), value_rows.reshape(seq, QUARTER, 4 * n1)],
        axis=1,
    ).reshape(2 * n1, 4 * n1)
    halves = [
        part
        for matrix in (forward1, forward_re, forward_im, filter2, inverse2, inverse1)
        for part in split_np(matrix)
    ]
    return halves + [ct.astype(np.float32), st.astype(np.float32)]


def split(values):
    high = values.astype(BF16)
    return high, (values - high.astype(F32)).astype(BF16)


def dot3(a, b, dims=((1,), (0,))):
    def one(x, y):
        return lax.dot_general(x, y, (dims, ((), ())), preferred_element_type=F32)

    return one(a[0], b[0]) + one(a[0], b[1]) + one(a[1], b[0])


def build_kernel(dp, seq, channels, lanes, token_total):
    cc = CHUNK_CHANNELS
    width = cc * seq
    chunks = channels // width
    rows = QUARTER * lanes
    n1 = QUARTER * seq
    dp_rows = channels // dp
    half_rows = dp_rows // CORES
    chips = seq // CORES
    groups = chips // chunks
    piece = half_rows // groups
    pair_count = (chunks // 2) * cc
    assert pair_count == dp and groups * chunks == chips and piece * groups == half_rows
    scale = 1.0 / math.sqrt(token_total)

    def kernel(
        tok, w_in, filt, cot,
        f1h, f1l, frh, frl, fih, fil, g2h, g2l, i2h, i2l, i1h, i1l, ct, st,
        mixed, token_grad, weight_grad,
        wsend, wall, wh, wl, th, tl, tth, ttl, gate,
        fsend, frecv, bsend, brecv,
        ftmp, ffs, fall, spec,
        wg, sib, rsend, rrecv, rsum, precv, agsend, agrecv,
        w_s, w_r, ff_s, ff_r, fg_s, fg_r, fs, fr, bs, br,
        sib_s, sib_r, rs_s, rs_r, p_s, p_r, ag_s, ag_r,
    ):
        me_dp = lax.axis_index("dp")
        me = lax.axis_index("seq")
        core = lax.rem(me, CORES)
        chip = me // CORES
        sibling = chip * CORES + (CORES - 1 - core)

        def remote(src, dst, send, recv, d, s):
            return pltpu.make_async_remote_copy(
                src_ref=src, dst_ref=dst, send_sem=send, recv_sem=recv,
                device_id=(d, s), device_id_type=MESH,
            )

        def wait_bytes(ref, sem):
            pltpu.make_async_copy(ref, ref, sem).wait()

        barrier = pltpu.get_barrier_semaphore()

        @pl.loop(1, seq)
        def _(i):
            pl.semaphore_signal(
                barrier, inc=1, device_id=(me_dp, lax.rem(me + i, seq)), device_id_type=MESH
            )

        @pl.loop(1, dp)
        def _(i):
            pl.semaphore_signal(
                barrier, inc=1, device_id=(lax.rem(me_dp + i, dp), me), device_id_type=MESH
            )

        for q in range(chunks):
            wsend[q, :, 0:width] = w_in[:, q * width : (q + 1) * width]
            wsend[q, :, width : 2 * width] = w_in[
                :, channels + q * width : channels + (q + 1) * width
            ]

        pair_chunk = me_dp // cc
        pair_row = lax.rem(me_dp, cc)
        for part in range(2):
            begin = pl.multiple_of((2 * pair_chunk + part) * width, width)
            for j in range(QUARTER):
                ftmp[j] = filt[j * lanes : (j + 1) * lanes, pl.ds(begin, width)].T
            for j in range(QUARTER):
                ffs[pl.ds(part * QUARTER + j, seq, stride=2 * QUARTER), :] = ftmp[
                    j, pl.ds(pl.multiple_of(pair_row * seq, seq), seq), :
                ]

        pl.semaphore_wait(barrier, seq - 1 + dp - 1)

        def send_weights(q):
            pltpu.make_async_copy(
                wsend.at[q], wall.at[q, pl.ds(me_dp * dp_rows, dp_rows), :], w_r.at[q]
            ).start()

            @pl.loop(1, dp)
            def _(i):
                remote(
                    wsend.at[q],
                    wall.at[q, pl.ds(me_dp * dp_rows, dp_rows), :],
                    w_s.at[q], w_r.at[q], lax.rem(me_dp + i, dp), me,
                ).start()

        send_weights(0)
        eight = 2 * QUARTER
        pltpu.make_async_copy(
            ffs.at[pl.ds(me * eight, eight), :],
            fall.at[me_dp, pl.ds(me * eight, eight), :],
            ff_r,
        ).start()

        @pl.loop(1, seq)
        def _(i):
            target = lax.rem(me + i, seq)
            remote(
                ffs.at[pl.ds(target * eight, eight), :],
                fall.at[me_dp, pl.ds(me * eight, eight), :],
                ff_s, ff_r, me_dp, target,
            ).start()

        @pl.loop(1, chunks)
        def _(q):
            send_weights(q)

        token_values = tok[0]
        high, low = split(token_values)
        th[...] = high
        tl[...] = low
        for j in range(QUARTER):
            for k in range(chunks):
                block = tok[0, j * lanes : (j + 1) * lanes, k * width : (k + 1) * width].T
                high, low = split(block)
                tth[k * width : (k + 1) * width, j * lanes : (j + 1) * lanes] = high
                ttl[k * width : (k + 1) * width, j * lanes : (j + 1) * lanes] = low

        wait_bytes(fall.at[me_dp], ff_r)

        @pl.loop(1, dp)
        def _(i):
            remote(
                fall.at[me_dp], fall.at[me_dp], fg_s, fg_r, lax.rem(me_dp + i, dp), me
            ).start()

        def exchange(source, target_ref, q, send, recv):
            pltpu.make_async_copy(
                source.at[q, :, pl.ds(me * eight, eight), :],
                target_ref.at[q, :, pl.ds(me * eight, eight), :],
                recv.at[q],
            ).start()

            @pl.loop(1, seq)
            def _(i):
                target = lax.rem(me + i, seq)
                remote(
                    source.at[q, :, pl.ds(target * eight, eight), :],
                    target_ref.at[q, :, pl.ds(me * eight, eight), :],
                    send.at[q], recv.at[q], me_dp, target,
                ).start()

        @pl.loop(0, chunks)
        def _(q):
            wait_bytes(wall.at[q], w_r.at[q])
            w_high, w_low = split(wall[q])
            wh[q] = w_high
            wl[q] = w_low
            projected = dot3((th[...], tl[...]), (w_high, w_low))
            gates = projected[:, width:]
            gate[q] = gates
            conv_grad = cot[0, :, pl.ds(pl.multiple_of(q * width, width), width)] * gates
            for part, values in ((0, projected[:, :width]), (1, conv_grad)):
                for j in range(QUARTER):
                    turned = values[j * lanes : (j + 1) * lanes].T
                    for c in range(cc):
                        fsend[q, c, pl.ds(part * QUARTER + j, seq, stride=eight), :] = turned[
                            c * seq : (c + 1) * seq
                        ]
            exchange(fsend, frecv, q, fs, fr)

        cos_t = ct[...]
        sin_t = st[...]

        def columns(blocks):
            return jnp.concatenate(blocks, axis=1)

        def forward_first(blocks):
            out = dot3((f1h[...], f1l[...]), split(columns(blocks)))
            parts = []
            for c in range(cc):
                lane = out[:, c * lanes : (c + 1) * lanes]
                parts.append([lane[k * n1 : (k + 1) * n1] for k in range(4)])
            return parts

        wait_bytes(fall.at[0 : dp - 1], fg_r)

        @pl.loop(0, chunks // 2)
        def _(p):
            parts = forward_first([fall[p * cc + c] for c in range(cc)])
            for part in range(2):
                stacked = []
                for c in range(cc):
                    real, imag = parts[c][2 * part], parts[c][2 * part + 1]
                    if part == 1:
                        imag = -imag
                    stacked.append(
                        columns([real * cos_t + imag * sin_t, imag * cos_t - real * sin_t])
                    )
                spec[2 * p + part] = dot3(
                    split(jnp.concatenate(stacked, axis=0)), (g2h[...], g2l[...])
                )

        @pl.loop(0, chunks)
        def _(q):
            wait_bytes(frecv.at[q], fr.at[q])
            parts = forward_first([frecv[q, c] for c in range(cc)])
            re_in, im_in = [], []
            for c in range(cc):
                a, b, e, f = parts[c]
                a, b = a * cos_t + b * sin_t, b * cos_t - a * sin_t
                e, f = e * cos_t - f * sin_t, f * cos_t + e * sin_t
                re_in.append(columns([a - f, b - e]))
                im_in.append(columns([b + e, a + f]))
            real = dot3(split(jnp.concatenate(re_in, axis=0)), (frh[...], frl[...]))
            imag = dot3(split(jnp.concatenate(im_in, axis=0)), (fih[...], fil[...]))
            h_real = spec[q, :, :lanes]
            h_imag = spec[q, :, lanes:]
            product = columns([real * h_real - imag * h_imag, real * h_imag + imag * h_real])
            inner = dot3(split(product), (i2h[...], i2l[...]))
            out_in = []
            for c in range(cc):
                block = inner[c * n1 : (c + 1) * n1]
                g, h, g2, h2 = [block[:, k * lanes : (k + 1) * lanes] for k in range(4)]
                out_in.append(
                    jnp.concatenate(
                        [
                            g * cos_t - h * sin_t,
                            h * cos_t + g * sin_t,
                            g2 * cos_t + h2 * sin_t,
                            h2 * cos_t - g2 * sin_t,
                        ],
                        axis=0,
                    )
                )
            result = dot3((i1h[...], i1l[...]), split(columns(out_in)))
            for c in range(cc):
                bsend[q, c] = result[:, c * lanes : (c + 1) * lanes]
            exchange(bsend, brecv, q, bs, br)

        def reduce_dp(q):
            wait_bytes(sib.at[q], sib_r.at[q])
            total = wg[q, :, core] + sib[q]
            rsend[q] = total
            pltpu.make_async_copy(rsend.at[q, me_dp], rrecv.at[q, me_dp], rs_r.at[q]).start()

            @pl.loop(1, dp)
            def _(i):
                target = lax.rem(me_dp + i, dp)
                remote(
                    rsend.at[q, target], rrecv.at[q, me_dp],
                    rs_s.at[q], rs_r.at[q], target, me,
                ).start()

        def sum_dp(q):
            wait_bytes(rrecv.at[q], rs_r.at[q])
            total = rrecv[q, 0]
            for k in range(1, dp):
                total = total + rrecv[q, k]
            rsum[pl.ds(q * groups, groups)] = total.reshape(groups, piece, 2 * width)

        @pl.loop(0, chunks)
        def _(q):
            wait_bytes(brecv.at[q], br.at[q])
            results = []
            for part in range(2):
                blocks = []
                for j in range(QUARTER):
                    turned = jnp.concatenate(
                        [
                            brecv[q, c, pl.ds(part * QUARTER + j, seq, stride=eight), :]
                            for c in range(cc)
                        ],
                        axis=0,
                    )
                    blocks.append(turned.T)
                results.append(jnp.concatenate(blocks, axis=0))
            convolved, d_value = results
            lane = pl.ds(pl.multiple_of(q * width, width), width)
            mixed[0, :, lane] = gate[q] * convolved
            d_pre = split(columns([d_value, cot[0, :, lane] * convolved]))
            grad = dot3((tth[...], ttl[...]), d_pre)
            wg[q] = grad.reshape(dp, CORES, half_rows, 2 * width)
            remote(
                wg.at[q, :, CORES - 1 - core], sib.at[q],
                sib_s.at[q], sib_r.at[q], me_dp, sibling,
            ).start()
            back = dot3(d_pre, (wh[q], wl[q]), ((1,), (1,)))

            @pl.when(q == 0)
            def _():
                token_grad[0] = back

            @pl.when(q > 0)
            def _():
                token_grad[0] = token_grad[0] + back

            reduce_dp(q)

        @pl.loop(0, chunks)
        def _(q):
            sum_dp(q)

        pltpu.make_async_copy(rsum.at[chip], precv.at[chip], p_r).start()

        @pl.loop(1, chips)
        def _(i):
            target = lax.rem(chip + i, chips)
            remote(
                rsum.at[target], precv.at[chip], p_s, p_r, me_dp, target * CORES + core
            ).start()

        wait_bytes(precv, p_r)
        total = precv[0]
        for k in range(1, chips):
            total = total + precv[k]
        agsend[...] = total * scale
        pltpu.make_async_copy(agsend, agrecv.at[me], ag_r).start()

        @pl.loop(1, seq)
        def _(i):
            remote(agsend, agrecv.at[me], ag_s, ag_r, me_dp, lax.rem(me + i, seq)).start()

        wait_bytes(agrecv, ag_r)
        for s in range(seq):
            q, g = (s // CORES) // groups, (s // CORES) % groups
            row = (s % CORES) * half_rows + g * piece
            got = agrecv[s]
            weight_grad[row : row + piece, q * width : (q + 1) * width] = got[:, :width]
            weight_grad[
                row : row + piece, channels + q * width : channels + (q + 1) * width
            ] = got[:, width:]

        @pl.loop(0, chunks)
        def _(q):
            wait_bytes(wall.at[q, 0 : (dp - 1) * dp_rows, :], w_s.at[q])
            wait_bytes(fsend.at[q, :, 0 : (seq - 1) * eight, :], fs.at[q])
            wait_bytes(bsend.at[q, :, 0 : (seq - 1) * eight, :], bs.at[q])
            wait_bytes(sib.at[q], sib_s.at[q])
            wait_bytes(rsend.at[q, 0 : dp - 1], rs_s.at[q])

        wait_bytes(ffs.at[0 : (seq - 1) * eight, :], ff_s)
        wait_bytes(fall.at[0 : dp - 1], fg_s)
        wait_bytes(rsum.at[0 : chips - 1], p_s)
        wait_bytes(agrecv.at[0 : seq - 1], ag_s)

    dma = pltpu.SemaphoreType.DMA
    f32, bf16 = F32, BF16
    scratch = [
        pltpu.VMEM((chunks, dp_rows, 2 * width), f32),
        pltpu.VMEM((chunks, channels, 2 * width), f32),
        pltpu.VMEM((chunks, channels, 2 * width), bf16),
        pltpu.VMEM((chunks, channels, 2 * width), bf16),
        pltpu.VMEM((rows, channels), bf16),
        pltpu.VMEM((rows, channels), bf16),
        pltpu.VMEM((channels, rows), bf16),
        pltpu.VMEM((channels, rows), bf16),
        pltpu.VMEM((chunks, rows, width), f32),
        pltpu.VMEM((chunks, cc, 2 * n1, lanes), f32),
        pltpu.VMEM((chunks, cc, 2 * n1, lanes), f32),
        pltpu.VMEM((chunks, cc, 2 * n1, lanes), f32),
        pltpu.VMEM((chunks, cc, 2 * n1, lanes), f32),
        pltpu.VMEM((QUARTER, width, lanes), f32),
        pltpu.VMEM((2 * n1, lanes), f32),
        pltpu.VMEM((dp, 2 * n1, lanes), f32),
        pltpu.VMEM((chunks, cc * n1, 2 * lanes), f32),
        pltpu.VMEM((chunks, dp, CORES, half_rows, 2 * width), f32),
        pltpu.VMEM((chunks, dp, half_rows, 2 * width), f32),
        pltpu.VMEM((chunks, dp, half_rows, 2 * width), f32),
        pltpu.VMEM((chunks, dp, half_rows, 2 * width), f32),
        pltpu.VMEM((chips, piece, 2 * width), f32),
        pltpu.VMEM((chips, piece, 2 * width), f32),
        pltpu.VMEM((piece, 2 * width), f32),
        pltpu.VMEM((seq, piece, 2 * width), f32),
        dma((chunks,)), dma((chunks,)), dma, dma, dma, dma,
        dma((chunks,)), dma((chunks,)), dma((chunks,)), dma((chunks,)),
        dma((chunks,)), dma((chunks,)), dma((chunks,)), dma((chunks,)),
        dma, dma, dma, dma,
    ]
    return kernel, scratch


def shards(dp, seq, tokens, in_weight, filters, cotangent):
    _, rows, channels = tokens.shape
    lanes = rows // QUARTER
    constants = tables(seq, lanes)
    kernel, scratch = build_kernel(dp, seq, channels, lanes, dp * seq * rows)
    whole = pl.BlockSpec(memory_space=pltpu.VMEM)
    return pl.pallas_call(
        kernel,
        out_shape=(
            jax.ShapeDtypeStruct(tokens.shape, F32),
            jax.ShapeDtypeStruct(tokens.shape, F32),
            jax.ShapeDtypeStruct(in_weight.shape, F32),
        ),
        in_specs=[whole] * (4 + len(constants)),
        out_specs=(whole,) * 3,
        scratch_shapes=scratch,
        compiler_params=pltpu.CompilerParams(
            collective_id=0, has_side_effects=True, vmem_limit_bytes=60 * 1024 * 1024
        ),
        name="gated_conv_layer",
    )(tokens, in_weight, filters, cotangent, *[jnp.asarray(c) for c in constants])


def solution(mesh):
    dp, seq = mesh.shape["dp"], mesh.shape["seq"]

    def local(tokens, in_weight, filters, cotangent):
        return shards(dp, seq, tokens, in_weight, filters, cotangent)

    placed = (P("dp", "seq", None), P("dp", None), P("seq", None), P("dp", "seq", None))
    return jax.shard_map(
        local,
        mesh=mesh,
        in_specs=placed,
        out_specs=(P("dp", "seq", None), P("dp", "seq", None), P("dp", None)),
        check_vma=False,
    )
```

time: 866 us -> 171 us (0.20)
  waiting for transfers between devices: 617 us -> 0 us
  Pallas kernels: 0 us -> 166 us
  matrix products: 76.7 us -> 0 us
  blocking collectives: 56.9 us -> 0 us
  local copies, waits for them, and re-layouts: 40.1 us -> 4.15 us
  other arithmetic: 33.7 us -> 0 us
  starting transfers between devices: 20.9 us -> 0 us
  between operations: 14.2 us -> 0.65 us
    psum x1 -> x0, waiting for transfers between devices: 265 us -> none  [shards(): grad_total = lax.psum(grad_shard, 'seq')]
    all_to_all x3 -> x0, waiting for transfers between devices: 244 us -> none  [the longest x1 120 us: forward_spread(): lax.all_to_all(moved, 'seq', split_axis=2, concat_axis=3, tiled=True)]
    pallas_call x0 -> x1, Pallas kernels: none -> 166 us  [shards(): pl.pallas_call(kernel, out_shape=(jax.ShapeDtypeStruct(tokens.shape, F32)...]
    dot_general x7 -> x0, matrix products: 76.7 us -> none  [the longest x2 47.6 us: local_transform(): return jnp.einsum('akbm,bjmc->ajkc', matrix, signal, precision=precise)]
    all_gather x1 -> x0, waiting for transfers between devices: 58.7 us -> none  [shards(): weights = lax.all_gather(in_weight, 'dp', axis=0, tiled=True)]
    all_to_all x1 -> x0, blocking collectives: 56.9 us -> none  [inverse_spread(): lax.all_to_all(moved, 'seq', split_axis=2, concat_axis=3, tiled=True)]
    unnamed x4 -> x0, waiting for transfers between devices: 49.8 us -> none
    all_to_all x3 -> x0, starting transfers between devices: 20.8 us -> none  [the longest x1 10.9 us: forward_spread(): lax.all_to_all(signal[:, None], 'seq', split_axis=2, concat_axis=1, tiled...]
  transfers between devices with their start and end apart: 6 -> 0, of which waited for: 6 -> 0; matrix products, arithmetic and copies ran while one was open for 3% -> 0% of each run, Pallas kernels for 0% -> 0%
where the time goes in v1:
time: 171 us
  Pallas kernels  166 us (97%)
  local copies, waits for them, and re-layouts  4.15 us (2%)
    pallas_call x1, Pallas kernels, shards(): pl.pallas_call(kernel, out_shape=(jax.ShapeDtypeStruct(tokens.shape, F32)...  166 us
    unnamed x7, local copies, waits for them, and re-layouts  4.15 us

profile of v1, /device:TPU:1, one launch (start us, length us, event | category | flops | bytes accessed | tf_op | source)
XLA Modules:
  0.0 171.3 jit_solution(4259263012134499304)
XLA Ops:
  0.6 166.5 %gated_conv_layer.1 = (f32[1,512,512]{2,1,0:T(8,128)}, f32[1,512,512]{2,1,0:T(8,128)}, f32[64,1024]{1,0:T(8,128)}) custom-call(f32[1,512,512]{2,1,0:T(8,128)} %tok.1, f32[64,1024]{1,0:T(8,128)} %w_in.1, f32[512,512]{1,0:T(8,128)} %filt.1, f32[1,512,512]{2,1,0:T(8,128)} %cot.1, bf16[512,256]{1,0:T(8,128)(2,1)} %constant.28.clone.f1h, ...), custom_call_target="tpu_custom_call" | custom-call | tf_op jit(solution)/shard_map/gated_conv_layer/pallas_call | solution.py:454
  167.1 0.0 copy-start
  167.1 2.4 %copy.24 = f32[1,512,512]{2,1,0:T(8,128)} copy(f32[1,512,512]{2,1,0:T(8,128)} %get-tuple-element.6) | data formatting | bytes 2097152
  169.5 0.0 copy-done
  169.5 0.0 copy-start.1
  169.5 1.0 copy.25
  170.5 0.1 copy-done.1
  170.6 0.7 copy.26
Async XLA Ops:
  167.1 2.4 %copy-start = (f32[1,512,512]{2,1,0:T(8,128)S(1)}, f32[1,512,512]{2,1,0:T(8,128)}, u32[]{:S(2)}) copy-start(f32[1,512,512]{2,1,0:T(8,128)} %get-tuple-element.7) | copy-start | bytes 3145732
  169.5 1.1 copy-start.1

commit v2 on v1

--- a/solution.py
+++ b/solution.py
@@ -13,6 +13,8 @@
 MESH = pl.DeviceIdType.MESH
 CORES = 2
 QUARTER = 4
+FILTER_SEND = 1
+FILTER_FORWARD = 2
 CHUNK_CHANNELS = 4
 
 
@@ -72,7 +74,7 @@
     return one(a[0], b[0]) + one(a[0], b[1]) + one(a[1], b[0])
 
 
-def build_kernel(dp, seq, channels, lanes, token_total):
+def build_kernel(dp, seq, channels, lanes, token_total, table_shapes):
     cc = CHUNK_CHANNELS
     width = cc * seq
     chunks = channels // width
@@ -81,28 +83,36 @@
     dp_rows = channels // dp
     half_rows = dp_rows // CORES
     chips = seq // CORES
-    groups = chips // chunks
+    rounds = chunks // 2
+    groups = chips // 4
     piece = half_rows // groups
-    pair_count = (chunks // 2) * cc
-    assert pair_count == dp and groups * chunks == chips and piece * groups == half_rows
+    assert rounds * cc == dp and groups * 4 == chips and piece * groups == half_rows
     scale = 1.0 / math.sqrt(token_total)
 
     def kernel(
-        tok, w_in, filt, cot,
+        tok_hbm, w_hbm, filt_hbm, cot_hbm,
+        f1h_x, f1l_x, frh_x, frl_x, fih_x, fil_x, g2h_x, g2l_x,
+        i2h_x, i2l_x, i1h_x, i1l_x, ct_x, st_x,
+        mixed_hbm, token_grad_hbm, weight_grad_hbm,
         f1h, f1l, frh, frl, fih, fil, g2h, g2l, i2h, i2l, i1h, i1l, ct, st,
-        mixed, token_grad, weight_grad,
-        wsend, wall, wh, wl, th, tl, tth, ttl, gate,
+        tok, w_in, filt, cot, mixed, token_grad, weight_grad,
+        wall, wh, wl, th, tl, tth, ttl, gate,
         fsend, frecv, bsend, brecv,
         ftmp, ffs, fall, spec,
         wg, sib, rsend, rrecv, rsum, precv, agsend, agrecv,
-        w_s, w_r, ff_s, ff_r, fg_s, fg_r, fs, fr, bs, br,
+        in_s, table_s, mixed_s, out_s,
+        wy_s, wy_r, wx_s, wx_r, wc_s, wc_r, ff_s, ff_r, fy_s, fy_r, fg_s, fg_r, fs, fr, bs, br,
         sib_s, sib_r, rs_s, rs_r, p_s, p_r, ag_s, ag_r,
     ):
         me_dp = lax.axis_index("dp")
         me = lax.axis_index("seq")
         core = lax.rem(me, CORES)
         chip = me // CORES
-        sibling = chip * CORES + (CORES - 1 - core)
+        other = CORES - 1 - core
+        sibling = chip * CORES + other
+        column = me_dp // 2
+        row = lax.rem(me_dp, 2)
+        partner = column * 2 + 1 - row
 
         def remote(src, dst, send, recv, d, s):
             return pltpu.make_async_remote_copy(
@@ -113,6 +123,27 @@
         def wait_bytes(ref, sem):
             pltpu.make_async_copy(ref, ref, sem).wait()
 
+        pair_chunk = me_dp // cc
+        pair_row = lax.rem(me_dp, cc)
+        begin = pl.multiple_of(2 * pair_chunk * width, width)
+        inputs = [
+            pltpu.make_async_copy(w_hbm, w_in, in_s.at[0]),
+            pltpu.make_async_copy(filt_hbm.at[:, pl.ds(begin, 2 * width)], filt, in_s.at[1]),
+            pltpu.make_async_copy(tok_hbm.at[0], tok, in_s.at[2]),
+            pltpu.make_async_copy(cot_hbm.at[0], cot, in_s.at[3]),
+        ]
+        sources = [
+            f1h_x, f1l_x, frh_x, frl_x, fih_x, fil_x, g2h_x, g2l_x,
+            i2h_x, i2l_x, i1h_x, i1l_x, ct_x, st_x,
+        ]
+        targets = [f1h, f1l, frh, frl, fih, fil, g2h, g2l, i2h, i2l, i1h, i1l, ct, st]
+        constants = [
+            pltpu.make_async_copy(source, target, table_s.at[k])
+            for k, (source, target) in enumerate(zip(sources, targets))
+        ]
+        for copy in inputs + constants:
+            copy.start()
+
         barrier = pltpu.get_barrier_semaphore()
 
         @pl.loop(1, seq)
@@ -127,39 +158,60 @@
                 barrier, inc=1, device_id=(lax.rem(me_dp + i, dp), me), device_id_type=MESH
             )
 
+        inputs[0].wait()
         for q in range(chunks):
-            wsend[q, :, 0:width] = w_in[:, q * width : (q + 1) * width]
-            wsend[q, :, width : 2 * width] = w_in[
-                :, channels + q * width : channels + (q + 1) * width
-            ]
-
-        pair_chunk = me_dp // cc
-        pair_row = lax.rem(me_dp, cc)
+            for h in range(2):
+                begin = h * channels + q * width
+                wall[q, me_dp, core, :, h * width : (h + 1) * width] = w_in[
+                    pl.ds(pl.multiple_of(core * half_rows, 8), half_rows), begin : begin + width
+                ]
+
+        pl.semaphore_wait(barrier, seq - 1 + dp - 1)
+
+        def send_along(block, send, recv):
+            @pl.loop(1, dp // 2)
+            def _(i):
+                target = lax.rem(column + i, dp // 2) * 2 + row
+                remote(block, block, send, recv, target, me).start()
+
+        def weights_pair(q):
+            block = wall.at[q, me_dp, core]
+            remote(block, block, wy_s.at[q], wy_r.at[q], partner, me).start()
+
+        def weights_own(q):
+            send_along(wall.at[q, me_dp, core], wx_s.at[q], wx_r.at[q])
+
+        def weights_forward(q):
+            block = wall.at[q, partner, core]
+            wait_bytes(block, wy_r.at[q])
+            send_along(block, wx_s.at[q], wx_r.at[q])
+
+        def weights_share(q):
+            wait_bytes(wall.at[q, 0 : dp - 2, 0], wx_r.at[q])
+            block = wall.at[q, :, core]
+            remote(block, block, wc_s.at[q], wc_r.at[q], me_dp, sibling).start()
+
+        weights_pair(0)
+        weights_own(0)
+
+        @pl.loop(1, chunks)
+        def _(q):
+            weights_pair(q)
+
+        inputs[1].wait()
         for part in range(2):
-            begin = pl.multiple_of((2 * pair_chunk + part) * width, width)
             for j in range(QUARTER):
-                ftmp[j] = filt[j * lanes : (j + 1) * lanes, pl.ds(begin, width)].T
+                ftmp[j] = filt[
+                    j * lanes : (j + 1) * lanes, part * width : (part + 1) * width
+                ].T
             for j in range(QUARTER):
                 ffs[pl.ds(part * QUARTER + j, seq, stride=2 * QUARTER), :] = ftmp[
                     j, pl.ds(pl.multiple_of(pair_row * seq, seq), seq), :
                 ]
 
-        pl.semaphore_wait(barrier, seq - 1 + dp - 1)
-
-        def send_weights(q):
-            pltpu.make_async_copy(
-                wsend.at[q], wall.at[q, pl.ds(me_dp * dp_rows, dp_rows), :], w_r.at[q]
-            ).start()
-
-            @pl.loop(1, dp)
-            def _(i):
-                remote(
-                    wsend.at[q],
-                    wall.at[q, pl.ds(me_dp * dp_rows, dp_rows), :],
-                    w_s.at[q], w_r.at[q], lax.rem(me_dp + i, dp), me,
-                ).start()
-
-        send_weights(0)
+        weights_forward(0)
+        weights_own(1)
+        weights_forward(1)
         eight = 2 * QUARTER
         pltpu.make_async_copy(
             ffs.at[pl.ds(me * eight, eight), :],
@@ -176,28 +228,12 @@
                 ff_s, ff_r, me_dp, target,
             ).start()
 
-        @pl.loop(1, chunks)
-        def _(q):
-            send_weights(q)
-
-        token_values = tok[0]
-        high, low = split(token_values)
+        inputs[2].wait()
+        high, low = split(tok[...])
         th[...] = high
         tl[...] = low
-        for j in range(QUARTER):
-            for k in range(chunks):
-                block = tok[0, j * lanes : (j + 1) * lanes, k * width : (k + 1) * width].T
-                high, low = split(block)
-                tth[k * width : (k + 1) * width, j * lanes : (j + 1) * lanes] = high
-                ttl[k * width : (k + 1) * width, j * lanes : (j + 1) * lanes] = low
-
-        wait_bytes(fall.at[me_dp], ff_r)
-
-        @pl.loop(1, dp)
-        def _(i):
-            remote(
-                fall.at[me_dp], fall.at[me_dp], fg_s, fg_r, lax.rem(me_dp + i, dp), me
-            ).start()
+        inputs[3].wait()
+        weights_share(0)
 
         def exchange(source, target_ref, q, send, recv):
             pltpu.make_async_copy(
@@ -217,14 +253,14 @@
 
         @pl.loop(0, chunks)
         def _(q):
-            wait_bytes(wall.at[q], w_r.at[q])
-            w_high, w_low = split(wall[q])
+            wait_bytes(wall.at[q, :, other], wc_r.at[q])
+            w_high, w_low = split(wall[q].reshape(channels, 2 * width))
             wh[q] = w_high
             wl[q] = w_low
             projected = dot3((th[...], tl[...]), (w_high, w_low))
             gates = projected[:, width:]
             gate[q] = gates
-            conv_grad = cot[0, :, pl.ds(pl.multiple_of(q * width, width), width)] * gates
+            conv_grad = cot[:, pl.ds(pl.multiple_of(q * width, width), width)] * gates
             for part, values in ((0, projected[:, :width]), (1, conv_grad)):
                 for j in range(QUARTER):
                     turned = values[j * lanes : (j + 1) * lanes].T
@@ -232,8 +268,39 @@
                         fsend[q, c, pl.ds(part * QUARTER + j, seq, stride=eight), :] = turned[
                             c * seq : (c + 1) * seq
                         ]
+
+            @pl.when(q < chunks - 1)
+            def _():
+                weights_share(q + 1)
+
+            @pl.when(q < chunks - 2)
+            def _():
+                weights_own(q + 2)
+                weights_forward(q + 2)
+
+            @pl.when(q == FILTER_SEND)
+            def _():
+                wait_bytes(fall.at[me_dp], ff_r)
+                block = fall.at[me_dp]
+                remote(block, block, fy_s, fy_r, partner, me).start()
+                send_along(block, fg_s, fg_r)
+
+            @pl.when(q == FILTER_FORWARD)
+            def _():
+                wait_bytes(fall.at[partner], fy_r)
+                send_along(fall.at[partner], fg_s, fg_r)
+
             exchange(fsend, frecv, q, fs, fr)
 
+        for j in range(QUARTER):
+            for k in range(chunks):
+                block = tok[j * lanes : (j + 1) * lanes, k * width : (k + 1) * width].T
+                high, low = split(block)
+                tth[k * width : (k + 1) * width, j * lanes : (j + 1) * lanes] = high
+                ttl[k * width : (k + 1) * width, j * lanes : (j + 1) * lanes] = low
+
+        for copy in constants:
+            copy.wait()
         cos_t = ct[...]
         sin_t = st[...]
 
@@ -248,7 +315,7 @@
                 parts.append([lane[k * n1 : (k + 1) * n1] for k in range(4)])
             return parts
 
-        wait_bytes(fall.at[0 : dp - 1], fg_r)
+        wait_bytes(fall.at[0 : dp - 2], fg_r)
 
         @pl.loop(0, chunks // 2)
         def _(p):
@@ -301,7 +368,10 @@
             result = dot3((i1h[...], i1l[...]), split(columns(out_in)))
             for c in range(cc):
                 bsend[q, c] = result[:, c * lanes : (c + 1) * lanes]
-            exchange(bsend, brecv, q, bs, br)
+
+            @pl.when(q < 2)
+            def _():
+                exchange(bsend, brecv, q, bs, br)
 
         def reduce_dp(q):
             wait_bytes(sib.at[q], sib_r.at[q])
@@ -322,7 +392,37 @@
             total = rrecv[q, 0]
             for k in range(1, dp):
                 total = total + rrecv[q, k]
-            rsum[pl.ds(q * groups, groups)] = total.reshape(groups, piece, 2 * width)
+            for g in range(groups):
+                for h in range(2):
+                    rsum[q // 2, lax.rem(q, 2) * 2 * groups + 2 * g + h] = total[
+                        g * piece : (g + 1) * piece, h * width : (h + 1) * width
+                    ]
+
+        def scatter_seq(r):
+            pltpu.make_async_copy(rsum.at[r, chip], precv.at[r, chip], p_r.at[r]).start()
+
+            @pl.loop(1, chips)
+            def _(i):
+                target = lax.rem(chip + i, chips)
+                remote(
+                    rsum.at[r, target], precv.at[r, chip],
+                    p_s.at[r], p_r.at[r], me_dp, target * CORES + core,
+                ).start()
+
+        def gather_seq(r):
+            wait_bytes(precv.at[r], p_r.at[r])
+            total = precv[r, 0]
+            for k in range(1, chips):
+                total = total + precv[r, k]
+            agsend[r] = total * scale
+            pltpu.make_async_copy(agsend.at[r], agrecv.at[r, me], ag_r.at[r]).start()
+
+            @pl.loop(1, seq)
+            def _(i):
+                remote(
+                    agsend.at[r], agrecv.at[r, me],
+                    ag_s.at[r], ag_r.at[r], me_dp, lax.rem(me + i, seq),
+                ).start()
 
         @pl.loop(0, chunks)
         def _(q):
@@ -342,78 +442,94 @@
                 results.append(jnp.concatenate(blocks, axis=0))
             convolved, d_value = results
             lane = pl.ds(pl.multiple_of(q * width, width), width)
-            mixed[0, :, lane] = gate[q] * convolved
-            d_pre = split(columns([d_value, cot[0, :, lane] * convolved]))
+            d_pre = split(columns([d_value, cot[:, lane] * convolved]))
             grad = dot3((tth[...], ttl[...]), d_pre)
             wg[q] = grad.reshape(dp, CORES, half_rows, 2 * width)
             remote(
                 wg.at[q, :, CORES - 1 - core], sib.at[q],
                 sib_s.at[q], sib_r.at[q], me_dp, sibling,
             ).start()
+
+            @pl.when(q > 0)
+            def _():
+                reduce_dp(q - 1)
+
+            @pl.when(q < chunks - 2)
+            def _():
+                exchange(bsend, brecv, q + 2, bs, br)
+
+            mixed[q] = gate[q] * convolved
+            pltpu.make_async_copy(mixed.at[q], mixed_hbm.at[0, :, lane], mixed_s.at[q]).start()
             back = dot3(d_pre, (wh[q], wl[q]), ((1,), (1,)))
 
             @pl.when(q == 0)
             def _():
-                token_grad[0] = back
+                token_grad[...] = back
 
             @pl.when(q > 0)
             def _():
-                token_grad[0] = token_grad[0] + back
-
-            reduce_dp(q)
+                token_grad[...] = token_grad[...] + back
+
+        grad_copy = pltpu.make_async_copy(token_grad, token_grad_hbm.at[0], out_s.at[0])
+        grad_copy.start()
+        for r in range(rounds - 1):
+            sum_dp(2 * r)
+            sum_dp(2 * r + 1)
+            scatter_seq(r)
+        reduce_dp(chunks - 1)
+        for r in range(rounds - 1):
+            gather_seq(r)
+        sum_dp(chunks - 2)
+        sum_dp(chunks - 1)
+        scatter_seq(rounds - 1)
+        gather_seq(rounds - 1)
+        for r in range(rounds):
+            wait_bytes(agrecv.at[r], ag_r.at[r])
+            for s in range(seq):
+                p = s // CORES
+                q, g, h = 2 * r + p // (2 * groups), (p % (2 * groups)) // 2, p % 2
+                row = (s % CORES) * half_rows + g * piece
+                column = h * channels + q * width
+                weight_grad[row : row + piece, column : column + width] = agrecv[r, s]
+        weight_copy = pltpu.make_async_copy(weight_grad, weight_grad_hbm, out_s.at[1])
+        weight_copy.start()
 
         @pl.loop(0, chunks)
         def _(q):
-            sum_dp(q)
-
-        pltpu.make_async_copy(rsum.at[chip], precv.at[chip], p_r).start()
-
-        @pl.loop(1, chips)
-        def _(i):
-            target = lax.rem(chip + i, chips)
-            remote(
-                rsum.at[target], precv.at[chip], p_s, p_r, me_dp, target * CORES + core
-            ).start()
-
-        wait_bytes(precv, p_r)
-        total = precv[0]
-        for k in range(1, chips):
-            total = total + precv[k]
-        agsend[...] = total * scale
-        pltpu.make_async_copy(agsend, agrecv.at[me], ag_r).start()
-
-        @pl.loop(1, seq)
-        def _(i):
-            remote(agsend, agrecv.at[me], ag_s, ag_r, me_dp, lax.rem(me + i, seq)).start()
-
-        wait_bytes(agrecv, ag_r)
-        for s in range(seq):
-            q, g = (s // CORES) // groups, (s // CORES) % groups
-            row = (s % CORES) * half_rows + g * piece
-            got = agrecv[s]
-            weight_grad[row : row + piece, q * width : (q + 1) * width] = got[:, :width]
-            weight_grad[
-                row : row + piece, channels + q * width : channels + (q + 1) * width
-            ] = got[:, width:]
-
-        @pl.loop(0, chunks)
-        def _(q):
-            wait_bytes(wall.at[q, 0 : (dp - 1) * dp_rows, :], w_s.at[q])
+            wait_bytes(wall.at[q, 0, 0], wy_s.at[q])
+            wait_bytes(wall.at[q, 0 : dp - 2, 0], wx_s.at[q])
+            wait_bytes(wall.at[q, :, 0], wc_s.at[q])
             wait_bytes(fsend.at[q, :, 0 : (seq - 1) * eight, :], fs.at[q])
             wait_bytes(bsend.at[q, :, 0 : (seq - 1) * eight, :], bs.at[q])
             wait_bytes(sib.at[q], sib_s.at[q])
             wait_bytes(rsend.at[q, 0 : dp - 1], rs_s.at[q])
 
         wait_bytes(ffs.at[0 : (seq - 1) * eight, :], ff_s)
-        wait_bytes(fall.at[0 : dp - 1], fg_s)
-        wait_bytes(rsum.at[0 : chips - 1], p_s)
-        wait_bytes(agrecv.at[0 : seq - 1], ag_s)
+        wait_bytes(fall.at[0], fy_s)
+        wait_bytes(fall.at[0 : dp - 2], fg_s)
+        for r in range(rounds):
+            wait_bytes(rsum.at[r, 0 : chips - 1], p_s.at[r])
+            wait_bytes(agrecv.at[r, 0 : seq - 1], ag_s.at[r])
+
+        @pl.loop(0, chunks)
+        def _(q):
+            lane = pl.ds(pl.multiple_of(q * width, width), width)
+            pltpu.make_async_copy(mixed.at[q], mixed_hbm.at[0, :, lane], mixed_s.at[q]).wait()
+
+        grad_copy.wait()
+        weight_copy.wait()
 
     dma = pltpu.SemaphoreType.DMA
     f32, bf16 = F32, BF16
-    scratch = [
-        pltpu.VMEM((chunks, dp_rows, 2 * width), f32),
-        pltpu.VMEM((chunks, channels, 2 * width), f32),
+    scratch = [pltpu.VMEM(shape, kind) for shape, kind in table_shapes] + [
+        pltpu.VMEM((rows, channels), f32),
+        pltpu.VMEM((dp_rows, 2 * channels), f32),
+        pltpu.VMEM((rows, 2 * width), f32),
+        pltpu.VMEM((rows, channels), f32),
+        pltpu.VMEM((chunks, rows, width), f32),
+        pltpu.VMEM((rows, channels), f32),
+        pltpu.VMEM((dp_rows, 2 * channels), f32),
+        pltpu.VMEM((chunks, dp, CORES, half_rows, 2 * width), f32),
         pltpu.VMEM((chunks, channels, 2 * width), bf16),
         pltpu.VMEM((chunks, channels, 2 * width), bf16),
         pltpu.VMEM((rows, channels), bf16),
@@ -433,14 +549,16 @@
         pltpu.VMEM((chunks, dp, half_rows, 2 * width), f32),
         pltpu.VMEM((chunks, dp, half_rows, 2 * width), f32),
         pltpu.VMEM((chunks, dp, half_rows, 2 * width), f32),
-        pltpu.VMEM((chips, piece, 2 * width), f32),
-        pltpu.VMEM((chips, piece, 2 * width), f32),
-        pltpu.VMEM((piece, 2 * width), f32),
-        pltpu.VMEM((seq, piece, 2 * width), f32),
-        dma((chunks,)), dma((chunks,)), dma, dma, dma, dma,
+        pltpu.VMEM((rounds, chips, piece, width), f32),
+        pltpu.VMEM((rounds, chips, piece, width), f32),
+        pltpu.VMEM((rounds, piece, width), f32),
+        pltpu.VMEM((rounds, seq, piece, width), f32),
+        dma((4,)), dma((len(table_shapes),)), dma((chunks,)), dma((2,)),
+        dma((chunks,)), dma((chunks,)), dma((chunks,)), dma((chunks,)),
+        dma((chunks,)), dma((chunks,)), dma, dma, dma, dma, dma, dma,
         dma((chunks,)), dma((chunks,)), dma((chunks,)), dma((chunks,)),
         dma((chunks,)), dma((chunks,)), dma((chunks,)), dma((chunks,)),
-        dma, dma, dma, dma,
+        dma((rounds,)), dma((rounds,)), dma((rounds,)), dma((rounds,)),
     ]
     return kernel, scratch
 
@@ -449,8 +567,10 @@
     _, rows, channels = tokens.shape
     lanes = rows // QUARTER
     constants = tables(seq, lanes)
-    kernel, scratch = build_kernel(dp, seq, channels, lanes, dp * seq * rows)
-    whole = pl.BlockSpec(memory_space=pltpu.VMEM)
+    kernel, scratch = build_kernel(
+        dp, seq, channels, lanes, dp * seq * rows, [(c.shape, c.dtype) for c in constants]
+    )
+    whole = pl.BlockSpec(memory_space=pl.ANY)
     return pl.pallas_call(
         kernel,
         out_shape=(

time: 171 us -> 147 us (0.86)
  Pallas kernels: 166 us -> 142 us
    pallas_call x1, Pallas kernels: 166 us -> 142 us  [shards(): pl.pallas_call(kernel, out_shape=(jax.ShapeDtypeStruct(tokens.shape, F32)...]
where the time goes in v2:
time: 147 us
  Pallas kernels  142 us (97%)
  local copies, waits for them, and re-layouts  4.15 us (3%)
    pallas_call x1, Pallas kernels, shards(): pl.pallas_call(kernel, out_shape=(jax.ShapeDtypeStruct(tokens.shape, F32)...  142 us
    unnamed x7, local copies, waits for them, and re-layouts  4.15 us

profile of v2, /device:TPU:1, one launch (start us, length us, event | category | flops | bytes accessed | tf_op | source)
XLA Modules:
  0.0 147.0 jit_solution(10499051628098891816)
XLA Ops:
  0.6 142.2 %gated_conv_layer.1 = (f32[1,512,512]{2,1,0:T(8,128)}, f32[1,512,512]{2,1,0:T(8,128)}, f32[64,1024]{1,0:T(8,128)}) custom-call(f32[1,512,512]{2,1,0:T(8,128)} %tok_hbm.1, f32[64,1024]{1,0:T(8,128)} %w_hbm.1, f32[512,512]{1,0:T(8,128)} %filt_hbm.1, f32[1,512,512]{2,1,0:T(8,128)} %cot_hbm.1, bf16[512,256]{1,0:T(8,128)(2,1)} %constant.28.clone.f1h_x, ...), custom_call_target="tpu_custom_call" | custom-call | tf_op jit(solution)/shard_map/gated_conv_layer/pallas_call | solution.py:574
  142.9 0.0 copy-start
  142.9 2.4 %copy.24 = f32[1,512,512]{2,1,0:T(8,128)} copy(f32[1,512,512]{2,1,0:T(8,128)} %get-tuple-element.6) | data formatting | bytes 2097152
  145.2 0.0 copy-done
  145.2 0.0 copy-start.1
  145.2 1.0 copy.25
  146.2 0.1 copy-done.1
  146.3 0.7 copy.26
Async XLA Ops:
  142.9 2.4 %copy-start = (f32[1,512,512]{2,1,0:T(8,128)S(1)}, f32[1,512,512]{2,1,0:T(8,128)}, u32[]{:S(2)}) copy-start(f32[1,512,512]{2,1,0:T(8,128)} %get-tuple-element.7) | copy-start | bytes 3145732
  145.2 1.1 copy-start.1

commit v3 on v2

--- a/solution.py
+++ b/solution.py
@@ -15,6 +15,7 @@
 QUARTER = 4
 FILTER_SEND = 1
 FILTER_FORWARD = 2
+STEPS = 2
 CHUNK_CHANNELS = 4
 
 
@@ -472,17 +473,13 @@
 
         grad_copy = pltpu.make_async_copy(token_grad, token_grad_hbm.at[0], out_s.at[0])
         grad_copy.start()
-        for r in range(rounds - 1):
+        reduce_dp(chunks - 1)
+        for r in range(rounds):
             sum_dp(2 * r)
             sum_dp(2 * r + 1)
             scatter_seq(r)
-        reduce_dp(chunks - 1)
-        for r in range(rounds - 1):
+        for r in range(rounds):
             gather_seq(r)
-        sum_dp(chunks - 2)
-        sum_dp(chunks - 1)
-        scatter_seq(rounds - 1)
-        gather_seq(rounds - 1)
         for r in range(rounds):
             wait_bytes(agrecv.at[r], ag_r.at[r])
             for s in range(seq):
@@ -571,13 +568,20 @@
         dp, seq, channels, lanes, dp * seq * rows, [(c.shape, c.dtype) for c in constants]
     )
     whole = pl.BlockSpec(memory_space=pl.ANY)
-    return pl.pallas_call(
+    shapes = (
+        jax.ShapeDtypeStruct(tokens.shape, F32),
+        jax.ShapeDtypeStruct(tokens.shape, F32),
+        jax.ShapeDtypeStruct(in_weight.shape, F32),
+    )
+
+    def place(a, b, c, x, y, z):
+        x[...] = a[...]
+        y[...] = b[...]
+        z[...] = c[...]
+
+    results = pl.pallas_call(
         kernel,
-        out_shape=(
-            jax.ShapeDtypeStruct(tokens.shape, F32),
-            jax.ShapeDtypeStruct(tokens.shape, F32),
-            jax.ShapeDtypeStruct(in_weight.shape, F32),
-        ),
+        out_shape=shapes,
         in_specs=[whole] * (4 + len(constants)),
         out_specs=(whole,) * 3,
         scratch_shapes=scratch,
@@ -586,6 +590,20 @@
         ),
         name="gated_conv_layer",
     )(tokens, in_weight, filters, cotangent, *[jnp.asarray(c) for c in constants])
+    steps = STEPS
+    blocks = (
+        pl.BlockSpec((1, rows // steps, channels), lambda i: (0, i, 0)),
+        pl.BlockSpec((1, rows // steps, channels), lambda i: (0, i, 0)),
+        pl.BlockSpec((in_weight.shape[0] // steps, 2 * channels), lambda i: (i, 0)),
+    )
+    return pl.pallas_call(
+        place,
+        grid=(steps,),
+        out_shape=shapes,
+        in_specs=list(blocks),
+        out_specs=blocks,
+        name="place_results",
+    )(*results)
 
 
 def solution(mesh):

time: 147 us -> 143 us (0.973)
  local copies, waits for them, and re-layouts: 4.15 us -> 0 us
    unnamed x7 -> x0, local copies, waits for them, and re-layouts: 4.15 us -> none
    pallas_call x1 -> x2, Pallas kernels: 142 us -> 143 us  [the longest x1 140 us: shards(): pl.pallas_call(kernel, out_shape=shapes, in_specs=[whole] * (4 + len(cons...]
where the time goes in v3:
time: 143 us
  Pallas kernels  143 us (100%)
    pallas_call x1, Pallas kernels, shards(): pl.pallas_call(kernel, out_shape=shapes, in_specs=[whole] * (4 + len(cons...  140 us

profile of v3, /device:TPU:1, one launch (start us, length us, event | category | flops | bytes accessed | tf_op | source)
XLA Modules:
  0.0 143.4 jit_solution(14228813308495798671)
XLA Ops:
  0.6 140.0 %gated_conv_layer.1 = (f32[1,512,512]{2,1,0:T(8,128)}, f32[1,512,512]{2,1,0:T(8,128)}, f32[64,1024]{1,0:T(8,128)}) custom-call(f32[1,512,512]{2,1,0:T(8,128)} %tok_hbm.1, f32[64,1024]{1,0:T(8,128)} %w_hbm.1, f32[512,512]{1,0:T(8,128)} %filt_hbm.1, f32[1,512,512]{2,1,0:T(8,128)} %cot_hbm.1, bf16[512,256]{1,0:T(8,128)(2,1)} %constant.28.clone.f1h_x, ...), custom_call_target="tpu_custom_call" | custom-call | tf_op jit(solution)/shard_map/gated_conv_layer/pallas_call | solution.py:582
  140.7 2.7 %place_results.1 = (f32[1,512,512]{2,1,0:T(8,128)}, f32[1,512,512]{2,1,0:T(8,128)}, f32[64,1024]{1,0:T(8,128)}) custom-call(f32[1,512,512]{2,1,0:T(8,128)} %get-tuple-element.6.a, f32[1,512,512]{2,1,0:T(8,128)} %get-tuple-element.7.b, f32[64,1024]{1,0:T(8,128)} %get-tuple-element.8.c), custom_call_target="tpu_custom_call" | custom-call | tf_op jit(solution)/shard_map/place_results/pallas_call | solution.py:599

commit v4 on v3

--- a/solution.py
+++ b/solution.py
@@ -210,10 +210,16 @@
                     j, pl.ds(pl.multiple_of(pair_row * seq, seq), seq), :
                 ]
 
+        eight = 2 * QUARTER
         weights_forward(0)
         weights_own(1)
+        inputs[2].wait()
+        high, low = split(tok[...])
+        th[...] = high
+        tl[...] = low
+        inputs[3].wait()
+        weights_share(0)
         weights_forward(1)
-        eight = 2 * QUARTER
         pltpu.make_async_copy(
             ffs.at[pl.ds(me * eight, eight), :],
             fall.at[me_dp, pl.ds(me * eight, eight), :],
@@ -228,13 +234,6 @@
                 fall.at[me_dp, pl.ds(me * eight, eight), :],
                 ff_s, ff_r, me_dp, target,
             ).start()
-
-        inputs[2].wait()
-        high, low = split(tok[...])
-        th[...] = high
-        tl[...] = low
-        inputs[3].wait()
-        weights_share(0)
 
         def exchange(source, target_ref, q, send, recv):
             pltpu.make_async_copy(

time: 143 us -> 143 us (level)
  no operation moved by 1% of the time
where the time goes in v4:
time: 143 us
  Pallas kernels  142 us (99%)
    pallas_call x1, Pallas kernels, shards(): pl.pallas_call(kernel, out_shape=shapes, in_specs=[whole] * (4 + len(cons...  139 us

profile of v4, /device:TPU:1, one launch (start us, length us, event | category | flops | bytes accessed | tf_op | source)
XLA Modules:
  0.0 142.5 jit_solution(8395913376005562343)
XLA Ops:
  0.6 139.2 %gated_conv_layer.1 = (f32[1,512,512]{2,1,0:T(8,128)}, f32[1,512,512]{2,1,0:T(8,128)}, f32[64,1024]{1,0:T(8,128)}) custom-call(f32[1,512,512]{2,1,0:T(8,128)} %tok_hbm.1, f32[64,1024]{1,0:T(8,128)} %w_hbm.1, f32[512,512]{1,0:T(8,128)} %filt_hbm.1, f32[1,512,512]{2,1,0:T(8,128)} %cot_hbm.1, bf16[512,256]{1,0:T(8,128)(2,1)} %constant.28.clone.f1h_x, ...), custom_call_target="tpu_custom_call" | custom-call | tf_op jit(solution)/shard_map/gated_conv_layer/pallas_call | solution.py:581
  139.8 2.7 %place_results.1 = (f32[1,512,512]{2,1,0:T(8,128)}, f32[1,512,512]{2,1,0:T(8,128)}, f32[64,1024]{1,0:T(8,128)}) custom-call(f32[1,512,512]{2,1,0:T(8,128)} %get-tuple-element.6.a, f32[1,512,512]{2,1,0:T(8,128)} %get-tuple-element.7.b, f32[64,1024]{1,0:T(8,128)} %get-tuple-element.8.c), custom_call_target="tpu_custom_call" | custom-call | tf_op jit(solution)/shard_map/place_results/pallas_call | solution.py:598
